TPU v7x, 256 devices: a whole 4x4x8 slice. The times are simulated.
256 devices in a mesh: seq: 32 (over z, x), vocab: 8 (over y, core).
Axes of the slice: x: 4, y: 4, z: 8, core: 2. Of those that a mesh axis runs over, the one named last changes fastest.
Arguments:
- hidden: bfloat16 [512, 5120], P(('seq', 'vocab')), may hold values from -400 to 400
- norm_gain: float32 [5120], replicated, may hold values from 0.1 to 1.9
- head_weight: bfloat16 [5120, 131072], P(None, ('seq', 'vocab')), may hold values from -2 to 2
- teacher_logits: bfloat16 [1024, 32, 4096], P('seq', None, 'vocab'), may hold values from -12 to 300
- teacher_slot: int32 [512], replicated, may hold values from 0 to 1023, as said below
- valid_tokens: int32 [512], replicated, may hold values 0 or 1
Outputs:
- grad_hidden: bfloat16 [512, 5120], P(('seq', 'vocab'))
- grad_head: bfloat16 [5120, 131072], P(None, ('seq', 'vocab'))
Inputs may be any that keep to these rules, and one draw needn't show every extreme that they name: `teacher_slot`: rows use distinct slots; slots g * 32 to (g + 1) * 32 - 1 belong to sequence group g of the teacher's packing; at most 32 rows use one group's slots, and some group holds 32 in every draw.
All inputs are finite; a program needn't handle non-finite values.
Results may differ from a plain program's by a relative error of at most 0.02.
Values may be sent and summed in bfloat16 or wider, within the bound.
A program may use at most 128 MiB of HBM per device.

v0:
```python
import jax
import jax.numpy as jnp
from jax import lax
from jax.sharding import PartitionSpec as P

epsilon = 1e-06


def shards(hidden, norm_gain, head_weight, teacher_logits, teacher_slot, valid_tokens):
    widened = hidden.astype(jnp.float32)
    inv_rms = lax.rsqrt(jnp.mean(widened * widened, axis=1, keepdims=True) + epsilon)
    normed = widened * inv_rms
    features = (normed * norm_gain).astype(jnp.bfloat16)
    gathered = lax.all_gather(features, ("seq", "vocab"), axis=0, tiled=True)
    logits = jnp.dot(gathered, head_weight, preferred_element_type=jnp.float32)
    arrived = lax.all_to_all(teacher_logits, "seq", split_axis=1, concat_axis=0, tiled=True)
    slot_table = arrived.reshape(arrived.shape[0], arrived.shape[2])
    teacher = jnp.take(slot_table, teacher_slot, axis=0).astype(jnp.float32)
    student_top, teacher_top = lax.pmax(
        (jnp.max(logits, axis=1), jnp.max(teacher, axis=1)), ("seq", "vocab")
    )
    shifted = jnp.exp(logits - student_top[:, None])
    teacher_shifted = jnp.exp(teacher - teacher_top[:, None])
    student_total, cross_sum, teacher_total = lax.psum(
        (
            jnp.sum(shifted, axis=1),
            jnp.sum(shifted * (logits - teacher), axis=1),
            jnp.sum(teacher_shifted, axis=1),
        ),
        ("seq", "vocab"),
    )
    student_lse = (student_top + jnp.log(student_total))[:, None]
    teacher_lse = (teacher_top + jnp.log(teacher_total))[:, None]
    divergence = cross_sum[:, None] / student_total[:, None] - student_lse + teacher_lse
    student_prob = jnp.exp(logits - student_lse)
    log_gap = logits - student_lse - (teacher - teacher_lse)
    row_weight = valid_tokens.astype(jnp.float32)[:, None]
    logit_grad = (row_weight * student_prob * (log_gap - divergence)).astype(jnp.bfloat16)
    grad_head = lax.dot_general(
        gathered, logit_grad, (((0,), (0,)), ((), ())), preferred_element_type=jnp.float32
    ).astype(jnp.bfloat16)
    feature_grad = lax.psum_scatter(
        lax.dot_general(
            logit_grad, head_weight, (((1,), (1,)), ((), ())), preferred_element_type=jnp.float32
        ),
        ("seq", "vocab"),
        scatter_dimension=0,
        tiled=True,
    )
    norm_grad = feature_grad * norm_gain
    grad_hidden = inv_rms * (
        norm_grad - normed * jnp.mean(norm_grad * normed, axis=1, keepdims=True)
    )
    return (grad_hidden.astype(jnp.bfloat16), grad_head)


def solution(mesh):
    placed = (
        P(("seq", "vocab"), None),
        P(),
        P(None, ("seq", "vocab")),
        P("seq", None, "vocab"),
        P(),
        P(),
    )
    return jax.shard_map(
        shards,
        mesh=mesh,
        in_specs=placed,
        out_specs=(P(("seq", "vocab"), None), P(None, ("seq", "vocab"))),
        check_vma=False,
    )
```

profile of v0, /device:TPU:97, one launch (start us, length us, event | category | flops | bytes accessed | tf_op | source)
XLA Modules:
  0.0 599.2 jit_solution(9775091275247822466)
XLA Ops:
  7.2 0.9 fusion.17
  8.1 1.4 fusion.19
  9.6 2.8 copy.10
  12.3 9.7 %all-to-all-start = ((bf16[32,32,512]{2,0,1:T(8,128)(2,1)}), bf16[32,32,512]{2,0,1:T(8,128)(2,1)S(1)}, u32[]{:S(2)}, u32[]{:S(2)}) async-start(bf16[32,32,512]{2,0,1:T(8,128)(2,1)} %copy.10), calls=%async_computation | async-start | bytes 2097152 | tf_op jit(solution)/shard_map/all_to_all | solution.py:16
  22.1 0.0 all-reduce.5.cloned.1.call-start
  22.1 0.7 convert_element_type.22
  22.8 0.7 compare_select_fusion
  23.5 0.7 compare_and_fusion
  24.2 23.7 %all-to-all-done = bf16[32,32,512]{2,0,1:T(8,128)(2,1)S(1)} async-done(((bf16[32,32,512]{2,0,1:T(8,128)(2,1)}), bf16[32,32,512]{2,0,1:T(8,128)(2,1)S(1)}, u32[]{:S(2)}, u32[]{:S(2)}) %all-to-all-start) | async-done | bytes 1048608 | tf_op jit(solution)/shard_map/all_to_all | solution.py:16
  47.9 2.0 gather_fusion
  49.8 0.2 copy.11
  50.1 0.2 fusion.9
  50.2 80.9 %all-gather.3.cloned.1.call-done = bf16[256,2,5120]{2,1,0:T(2,128)(2,1)} async-done(((bf16[1,2,5120]{2,1,0:T(2,128)(2,1)}), bf16[256,2,5120]{2,1,0:T(2,128)(2,1)}) %all-gather.3.cloned.1.call-update) | async-done | bytes 5242896 | tf_op jit(solution)/shard_map/all_gather | solution.py:14
  131.1 11.5 %reshape.46 = bf16[512,5120]{1,0:T(8,128)(2,1)} reshape(bf16[256,2,5120]{2,1,0:T(2,128)(2,1)} %all-gather.3.cloned.1.call-done) | data formatting | bytes 10485760
  142.6 7.2 %fusion.20 = (f32[512]{0:T(512)S(1)}, f32[512,512]{0,1:T(8,128)S(1)}) fusion(bf16[512,5120]{1,0:T(8,128)(2,1)} %reshape.46, bf16[5120,512]{1,0:T(8,128)(2,1)} %param.8), kind=kOutput, calls=%fused_computation.38 | convolution fusion | flops 2684616192 | bytes 11536384 | tf_op jit(solution)/shard_map/dot_general | solution.py:15
  149.8 74.6 %all-reduce.2 = (f32[512]{0:T(512)S(1)}, f32[512]{0:T(512)S(1)}) all-reduce(bf16[512]{0:T(512)(128)(2,1)S(1)} %fusion.9, f32[512]{0:T(512)S(1)} %get-tuple-element.13), channel_id=1, replica_groups=mesh['seq'=32,'vocab'=8] {'seq','vocab'}, use_global_device_ids=true, to_apply=%region_6.7 | all-reduce | flops 1024 | bytes 7168 | tf_op jit(solution)/shard_map/pmax | solution.py:19
  224.4 0.5 fusion.8
  224.9 74.2 %all-reduce.1 = (f32[512]{0:T(512)S(1)}, f32[512]{0:T(512)S(1)}, f32[512]{0:T(512)S(1)}) all-reduce(f32[512]{0:T(512)S(1)} %get-tuple-element.4, f32[512]{0:T(512)S(1)} %get-tuple-element.3, f32[512]{0:T(512)S(1)} %get-tuple-element.2), channel_id=1, replica_groups=mesh['seq'=32,'vocab'=8] {'seq','vocab'}, use_global_device_ids=true, to_apply=%region_8.9 | all-reduce | flops 1536 | bytes 12288 | tf_op jit(solution)/shard_map/psum | solution.py:24
  299.1 0.4 fusion.5
  299.5 8.0 %fusion.21 = f32[512,5120]{1,0:T(8,128)} fusion(bf16[512,512]{0,1:T(8,128)(2,1)S(1)} %fusion.5, bf16[5120,512]{1,0:T(8,128)(2,1)} %param.8), kind=kOutput, calls=%fused_computation.39 | convolution fusion | flops 2684354560 | bytes 16252928 | tf_op jit(solution)/shard_map/dot_general | solution.py:43
  307.5 7.2 %convolution_convert_fusion = bf16[5120,512]{1,0:T(8,128)(2,1)} fusion(bf16[512,5120]{1,0:T(8,128)(2,1)} %reshape.46, bf16[512,512]{0,1:T(8,128)(2,1)S(1)} %fusion.5), kind=kOutput, calls=%fused_computation.1 | convolution fusion | flops 2686976000 | bytes 11010048 | tf_op jit(solution)/shard_map/dot_general | solution.py:39
  314.7 274.8 %all-reduce.5.cloned.1.call-done = f32[512,5120]{1,0:T(8,128)} async-done(((f32[512,5120]{1,0:T(8,128)}), f32[512,5120]{1,0:T(8,128)}) %all-reduce.5.cloned.1.call-update) | async-done | bytes 10485776
  589.5 1.1 fusion.14
  590.7 1.6 fusion.18
  (11 shorter events, 0.1 us)
Async XLA Ops:
  7.2 124.0 %all-gather.3.cloned.1.call-start = ((), (), s32[]{:S(2)}) async-start(), calls=%async_computation.1 | async-start | bytes 5263360 | tf_op jit(solution)/shard_map/all_gather | solution.py:14
  12.3 35.5 %all-to-all-start = ((bf16[32,32,512]{2,0,1:T(8,128)(2,1)}), bf16[32,32,512]{2,0,1:T(8,128)(2,1)S(1)}, u32[]{:S(2)}, u32[]{:S(2)}) async-start(bf16[32,32,512]{2,0,1:T(8,128)(2,1)} %copy.10), calls=%async_computation | async-start | bytes 2097152 | tf_op jit(solution)/shard_map/all_to_all | solution.py:16
  22.1 567.5 %all-reduce.5.cloned.1.call-start = ((), (), s32[]{:S(2)}) async-start(), calls=%async_computation.2 | async-start | bytes 20971520
  307.5 282.0 %copy-start = (bf16[2,5120]{1,0:T(2,128)(2,1)S(1)}, bf16[2,5120]{1,0:T(2,128)(2,1)}, u32[]{:S(2)}) copy-start(bf16[2,5120]{1,0:T(2,128)(2,1)} %param.6) | copy-start | bytes 61444
  307.5 282.0 %copy-start.1 = (f32[5120]{0:T(1024)S(1)}, f32[5120]{0:T(1024)}, u32[]{:S(2)}) copy-start(f32[5120]{0:T(1024)} %param.7) | copy-start | bytes 61444
Sparse Core Ops, SparseCore 0:
  12.3 118.8 all-gather.2
  307.6 281.8 all-reduce.4
where the time goes:
time: 600 us; the launch traced here: 599 us
  waiting for transfers between devices  379 us (63%)
  blocking collectives  149 us (25%)
  matrix products  22.3 us (4%)
  local copies, waits for them, and re-layouts  16.4 us (3%)
  between operations  14.1 us (2%)
  starting transfers between devices  9.8 us (2%)
  other arithmetic  8.17 us (1%)
    unnamed x3, waiting for transfers between devices  275 us
    all_gather x1, waiting for transfers between devices, shards(): gathered = lax.all_gather(features, ('seq', 'vocab'), axis=0, tiled=True)  80.9 us
    pmax x1, blocking collectives, shards(): lax.pmax((jnp.max(logits, axis=1), jnp.max(teacher, axis=1)), ('seq', 'vo...  74.6 us
    psum x1, blocking collectives, shards(): lax.psum((jnp.sum(shifted, axis=1), jnp.sum(shifted * (logits - teacher),...  74.2 us
    all_to_all x1, waiting for transfers between devices, shards(): lax.all_to_all(teacher_logits, 'seq', split_axis=1, concat_axis=0, tiled=...  23.7 us
    unnamed x6, local copies, waits for them, and re-layouts  14.2 us
  transfers between devices with their start and end apart: 3, of which 3 were waited for; matrix products, arithmetic and copies ran while one was open for 2% of the time, Pallas kernels for 0%

commit v1 on v0

--- a/solution.py
+++ b/solution.py
@@ -11,7 +11,12 @@
     inv_rms = lax.rsqrt(jnp.mean(widened * widened, axis=1, keepdims=True) + epsilon)
     normed = widened * inv_rms
     features = (normed * norm_gain).astype(jnp.bfloat16)
-    gathered = lax.all_gather(features, ("seq", "vocab"), axis=0, tiled=True)
+    gathered = jnp.concatenate(
+        lax.all_to_all(
+            jnp.stack([features] * lax.axis_size(("seq", "vocab"))), ("seq", "vocab"), 0, 0
+        ),
+        axis=0,
+    )
     logits = jnp.dot(gathered, head_weight, preferred_element_type=jnp.float32)
     arrived = lax.all_to_all(teacher_logits, "seq", split_axis=1, concat_axis=0, tiled=True)
     slot_table = arrived.reshape(arrived.shape[0], arrived.shape[2])

time: 600 us -> 649 us (1.082)
  waiting for transfers between devices: 379 us -> 412 us
  starting transfers between devices: 9.8 us -> 23.4 us
    all_to_all x0 -> x1, waiting for transfers between devices: none -> 113 us  [shards(): lax.all_to_all(jnp.stack([features] * lax.axis_size(('seq', 'vocab'))), (...]
    all_gather x1 -> x0, waiting for transfers between devices: 80.9 us -> none  [shards(): gathered = lax.all_gather(features, ('seq', 'vocab'), axis=0, tiled=True)]
    all_to_all x0 -> x1, starting transfers between devices: none -> 13.6 us  [shards(): lax.all_to_all(jnp.stack([features] * lax.axis_size(('seq', 'vocab'))), (...]
    reshape x0 -> x1, local copies, waits for them, and re-layouts: none -> 11.5 us  [shards(): jnp.concatenate(lax.all_to_all(jnp.stack([features] * lax.axis_size(('seq...]
    unnamed x6 -> x9, local copies, waits for them, and re-layouts: 14.2 us -> 2.79 us
    unnamed x3 -> x2, waiting for transfers between devices: 275 us -> 275 us
where the time goes in v1:
time: 649 us; the launch traced here: 648 us
  waiting for transfers between devices  412 us (63%)
  blocking collectives  150 us (23%)
  starting transfers between devices  23.4 us (4%)
  matrix products  22.4 us (3%)
  local copies, waits for them, and re-layouts  21.5 us (3%)
  between operations  14.1 us (2%)
    unnamed x2, waiting for transfers between devices  275 us
    all_to_all x1, waiting for transfers between devices, shards(): lax.all_to_all(jnp.stack([features] * lax.axis_size(('seq', 'vocab'))), (...  113 us
    pmax x1, blocking collectives, shards(): lax.pmax((jnp.max(logits, axis=1), jnp.max(teacher, axis=1)), ('seq', 'vo...  75.6 us
    psum x1, blocking collectives, shards(): lax.psum((jnp.sum(shifted, axis=1), jnp.sum(shifted * (logits - teacher),...  74.1 us
    all_to_all x1, waiting for transfers between devices, shards(): lax.all_to_all(teacher_logits, 'seq', split_axis=1, concat_axis=0, tiled=...  23.8 us
    all_to_all x1, starting transfers between devices, shards(): lax.all_to_all(jnp.stack([features] * lax.axis_size(('seq', 'vocab'))), (...  13.6 us
  transfers between devices with their start and end apart: 3, of which 3 were waited for; matrix products, arithmetic and copies ran while one was open for 2% of the time, Pallas kernels for 0%

profile of v1, /device:TPU:97, one launch (start us, length us, event | category | flops | bytes accessed | tf_op | source)
XLA Modules:
  0.0 648.2 jit_solution(939039543705293786)
XLA Ops:
  7.2 2.8 copy.10
  9.9 9.7 %all-to-all-start.1 = ((bf16[32,32,512]{2,0,1:T(8,128)(2,1)}), bf16[32,32,512]{2,0,1:T(8,128)(2,1)S(1)}, u32[]{:S(2)}, u32[]{:S(2)}) async-start(bf16[32,32,512]{2,0,1:T(8,128)(2,1)} %copy.10), calls=%async_computation.1 | async-start | bytes 2097152 | tf_op jit(solution)/shard_map/all_to_all | solution.py:21
  19.7 0.9 fusion.17
  20.6 0.8 fusion.13
  21.4 23.8 %all-to-all-done.1 = bf16[32,32,512]{2,0,1:T(8,128)(2,1)S(1)} async-done(((bf16[32,32,512]{2,0,1:T(8,128)(2,1)}), bf16[32,32,512]{2,0,1:T(8,128)(2,1)S(1)}, u32[]{:S(2)}, u32[]{:S(2)}) %all-to-all-start.1) | async-done | bytes 1048608 | tf_op jit(solution)/shard_map/all_to_all | solution.py:21
  45.2 5.1 stack.2
  50.2 13.6 %all-to-all-start = ((bf16[256,2,5120]{2,1,0:T(2,128)(2,1)}), bf16[256,2,5120]{2,1,0:T(2,128)(2,1)}, u32[]{:S(2)}, u32[]{:S(2)}) async-start(bf16[256,2,5120]{2,1,0:T(2,128)(2,1)} %stack.2), calls=%async_computation | async-start | bytes 10485760 | tf_op jit(solution)/shard_map/all_to_all | solution.py:15
  63.8 0.0 all-reduce.5.cloned.1.call-start
  64.0 2.0 gather_fusion
  65.9 0.2 copy.11
  66.2 0.2 fusion.9
  66.3 112.8 %all-to-all-done = bf16[256,2,5120]{2,1,0:T(2,128)(2,1)} async-done(((bf16[256,2,5120]{2,1,0:T(2,128)(2,1)}), bf16[256,2,5120]{2,1,0:T(2,128)(2,1)}, u32[]{:S(2)}, u32[]{:S(2)}) %all-to-all-start) | async-done | bytes 5242912 | tf_op jit(solution)/shard_map/all_to_all | solution.py:15
  179.1 11.5 %reshape.40 = bf16[512,5120]{1,0:T(8,128)(2,1)} reshape(bf16[256,2,5120]{2,1,0:T(2,128)(2,1)} %all-to-all-done) | data formatting | bytes 10485760 | tf_op jit(solution)/shard_map/reshape | solution.py:14
  190.6 7.2 %fusion.19 = (f32[512]{0:T(512)S(1)}, f32[512,512]{0,1:T(8,128)S(1)}) fusion(bf16[512,5120]{1,0:T(8,128)(2,1)} %reshape.40, bf16[5120,512]{1,0:T(8,128)(2,1)} %param.8), kind=kOutput, calls=%fused_computation.37 | convolution fusion | flops 2684616192 | bytes 11536384 | tf_op jit(solution)/shard_map/dot_general | solution.py:20
  197.8 75.6 %all-reduce.2 = (f32[512]{0:T(512)S(1)}, f32[512]{0:T(512)S(1)}) all-reduce(bf16[512]{0:T(512)(128)(2,1)S(1)} %fusion.9, f32[512]{0:T(512)S(1)} %get-tuple-element.13), channel_id=1, replica_groups=mesh['seq'=32,'vocab'=8] {'seq','vocab'}, use_global_device_ids=true, to_apply=%region_6.7 | all-reduce | flops 1024 | bytes 7168 | tf_op jit(solution)/shard_map/pmax | solution.py:24
  273.4 0.5 fusion.8
  273.8 74.1 %all-reduce.1 = (f32[512]{0:T(512)S(1)}, f32[512]{0:T(512)S(1)}, f32[512]{0:T(512)S(1)}) all-reduce(f32[512]{0:T(512)S(1)} %get-tuple-element.4, f32[512]{0:T(512)S(1)} %get-tuple-element.3, f32[512]{0:T(512)S(1)} %get-tuple-element.2), channel_id=1, replica_groups=mesh['seq'=32,'vocab'=8] {'seq','vocab'}, use_global_device_ids=true, to_apply=%region_8.9 | all-reduce | flops 1536 | bytes 12288 | tf_op jit(solution)/shard_map/psum | solution.py:29
  347.9 0.4 fusion.5
  348.3 8.0 %fusion.20 = f32[512,5120]{1,0:T(8,128)} fusion(bf16[512,512]{0,1:T(8,128)(2,1)S(1)} %fusion.5, bf16[5120,512]{1,0:T(8,128)(2,1)} %param.8), kind=kOutput, calls=%fused_computation.38 | convolution fusion | flops 2684354560 | bytes 16252928 | tf_op jit(solution)/shard_map/dot_general | solution.py:48
  356.3 0.0 all-reduce.5.cloned.1.call-update
  356.3 7.2 %convolution_convert_fusion = bf16[5120,512]{1,0:T(8,128)(2,1)} fusion(bf16[512,5120]{1,0:T(8,128)(2,1)} %reshape.40, bf16[512,512]{0,1:T(8,128)(2,1)S(1)} %fusion.5), kind=kOutput, calls=%fused_computation.1 | convolution fusion | flops 2686976000 | bytes 11010048 | tf_op jit(solution)/shard_map/dot_general | solution.py:44
  363.5 275.1 %all-reduce.5.cloned.1.call-done = f32[512,5120]{1,0:T(8,128)} async-done(((f32[512,5120]{1,0:T(8,128)}), f32[512,5120]{1,0:T(8,128)}) %all-reduce.5.cloned.1.call-update) | async-done | bytes 10485776
  638.6 1.1 fusion.14
  639.7 1.6 fusion.18
  (15 shorter events, 0.1 us)
Async XLA Ops:
  9.9 35.2 %all-to-all-start.1 = ((bf16[32,32,512]{2,0,1:T(8,128)(2,1)}), bf16[32,32,512]{2,0,1:T(8,128)(2,1)S(1)}, u32[]{:S(2)}, u32[]{:S(2)}) async-start(bf16[32,32,512]{2,0,1:T(8,128)(2,1)} %copy.10), calls=%async_computation.1 | async-start | bytes 2097152 | tf_op jit(solution)/shard_map/all_to_all | solution.py:21
  50.2 13.7 %copy-start.3 = (s32[512]{0:T(512)S(1)}, s32[512]{0:T(512)}, u32[]{:S(2)}) copy-start(s32[512]{0:T(512)} %param.11) | copy-start | bytes 6148
  50.2 13.7 %copy-start.2 = (s32[512]{0:T(512)S(1)}, s32[512]{0:T(512)}, u32[]{:S(2)}) copy-start(s32[512]{0:T(512)} %param.10) | copy-start | bytes 6148
  50.2 128.9 %all-to-all-start = ((bf16[256,2,5120]{2,1,0:T(2,128)(2,1)}), bf16[256,2,5120]{2,1,0:T(2,128)(2,1)}, u32[]{:S(2)}, u32[]{:S(2)}) async-start(bf16[256,2,5120]{2,1,0:T(2,128)(2,1)} %stack.2), calls=%async_computation | async-start | bytes 10485760 | tf_op jit(solution)/shard_map/all_to_all | solution.py:15
  63.8 574.7 %all-reduce.5.cloned.1.call-start = ((), (), s32[]{:S(2)}) async-start(), calls=%async_computation.2 | async-start | bytes 20971520
  356.3 282.3 %copy-start = (bf16[2,5120]{1,0:T(2,128)(2,1)S(1)}, bf16[2,5120]{1,0:T(2,128)(2,1)}, u32[]{:S(2)}) copy-start(bf16[2,5120]{1,0:T(2,128)(2,1)} %param.6) | copy-start | bytes 61444
  356.3 282.3 %copy-start.1 = (f32[5120]{0:T(1024)S(1)}, f32[5120]{0:T(1024)}, u32[]{:S(2)}) copy-start(f32[5120]{0:T(1024)} %param.7) | copy-start | bytes 61444
Sparse Core Ops, SparseCore 0:
  356.4 282.1 all-reduce.4
